TPU v7x, 32 devices: a whole 2x2x4 slice. The times are simulated.
32 devices in a mesh: dp: 4 (over y, x), fsdp: 8 (over z, core).
Axes of the slice: x: 2, y: 2, z: 4, core: 2. Of those that a mesh axis runs over, the one named last changes fastest.
Arguments:
- hidden: bfloat16 [32, 256, 5120], P(('dp', 'fsdp')), may hold values from -6 to 6
- queries: bfloat16 [32, 256, 1024], P(('dp', 'fsdp')), may hold values from -6 to 6
- upstream: bfloat16 [32, 256, 1024], P(('dp', 'fsdp')), may hold values from -0.3984375 to 0.3984375
- advantage: float32 [32, 256], P(('dp', 'fsdp')), may hold values from -5 to 5
- selected: int32 [32, 256], P(('dp', 'fsdp')), may hold values from 0 to 1, as said below
- segment: int32 [32, 256], P(('dp', 'fsdp')), may hold values from 0 to 3, never falling along the last dimension, each value on 1 to 128 neighbouring positions
- w_kv: bfloat16 [5120, 256], P('fsdp'), may hold values from -0.078125 to 0.078125
- k_gain: float32 [128], replicated, may hold values from 0.25 to 1.75
- q_gain: float32 [128], replicated, may hold values from 0.25 to 1.75
Outputs:
- d_weight: float32 [5120, 256], P('fsdp')
- d_gain: float32 [128], replicated
Inputs may be any that keep to these rules, and one draw needn't show every extreme that they name: Each row has at most 128 selected tokens, and some row has exactly 128.
All inputs are finite; a program needn't handle non-finite values.
Results may differ from a plain program's by a relative error of at most 0.007.
Values may be sent and summed in bfloat16 or wider, within the bound.
A program may use at most 64 MiB of HBM per device.

v0:
```python
import jax
import jax.numpy as jnp
from jax import lax
from jax.sharding import PartitionSpec as P

CAP = 128


epsilon = 1e-06


def attend(q_rows, g_rows, q_place, q_group, k_norm, values, k_place, k_group, score_scale):
    allowed = (q_group[:, None] == k_group[None, :]) & (k_place[None, :] <= q_place[:, None])
    scores = (
        jnp.einsum("qhd,kd->hqk", q_rows, k_norm, preferred_element_type=jnp.float32) * score_scale
    )
    expo = jnp.where(allowed[None], jnp.exp(scores), 0.0)
    probs = expo / jnp.sum(expo, axis=-1, keepdims=True)
    probs_b = probs.astype(jnp.bfloat16)
    outputs = jnp.einsum("hqk,kd->qhd", probs_b, values, preferred_element_type=jnp.float32)
    delta = jnp.sum(g_rows.astype(jnp.float32) * outputs, axis=-1)
    dprob = jnp.einsum("qhd,kd->hqk", g_rows, values, preferred_element_type=jnp.float32)
    dscore = (probs * (dprob - delta.T[:, :, None]) * score_scale).astype(jnp.bfloat16)
    d_key = jnp.einsum("hqk,qhd->kd", dscore, q_rows, preferred_element_type=jnp.float32)
    d_value = jnp.einsum("hqk,qhd->kd", probs_b, g_rows, preferred_element_type=jnp.float32)
    return (d_key, d_value)


def shards(hidden, queries, upstream, advantage, selected, segment, w_kv, k_gain, q_gain):
    hidden_row = hidden[0]
    length = hidden_row.shape[0]
    width = hidden_row.shape[1]
    rows_dev = w_kv.shape[0]
    head_dim = k_gain.shape[0]
    heads = queries.shape[2] // head_dim
    owners = lax.axis_size("fsdp")
    padded_width = rows_dev * owners
    hidden_pad = jnp.pad(hidden_row, ((0, 0), (0, padded_width - width)))
    columns = hidden_pad
    key_value = jnp.dot(
        columns,
        lax.all_gather(w_kv, "fsdp", axis=0, tiled=True),
        preferred_element_type=jnp.float32,
    )
    k_raw = key_value[:, :head_dim]
    k_scale = lax.rsqrt(jnp.mean(k_raw * k_raw, axis=-1, keepdims=True) + epsilon)
    k_hat = k_raw * k_scale
    k_norm = (k_hat * k_gain).astype(jnp.bfloat16)
    values = key_value[:, head_dim:].astype(jnp.bfloat16)
    query_full = queries[0].reshape(length, heads, head_dim).astype(jnp.float32)
    q_scale = lax.rsqrt(jnp.mean(query_full * query_full, axis=-1, keepdims=True) + epsilon)
    q_norm = (query_full * q_scale * q_gain).astype(jnp.bfloat16)
    token_weight = advantage[0] * selected[0].astype(jnp.float32)
    cotangent = (token_weight[:, None] * upstream[0].astype(jnp.float32)).astype(jnp.bfloat16)
    cotangent = cotangent.reshape(length, heads, head_dim)
    positions = jnp.arange(length, dtype=jnp.int32)
    segment_row = segment[0]
    score_scale = head_dim ** (-0.5)
    picked = jnp.nonzero(selected[0], size=CAP, fill_value=0)[0].astype(jnp.int32)
    filled = jnp.arange(CAP) < jnp.sum(selected[0])
    q_rows = q_norm[picked]
    g_rows = jnp.where(filled[:, None, None], cotangent[picked], jnp.zeros((), jnp.bfloat16))
    d_key, d_value = attend(
        q_rows,
        g_rows,
        positions[picked],
        segment_row[picked],
        k_norm,
        values,
        positions,
        segment_row,
        score_scale,
    )
    d_khat = d_key * k_gain
    gain_term = jnp.sum(d_key * k_hat, axis=0)
    d_kraw = k_scale * (d_khat - k_hat * jnp.mean(d_khat * k_hat, axis=-1, keepdims=True))
    d_kv = jnp.concatenate([d_kraw, d_value], axis=1).astype(jnp.bfloat16)
    columns = hidden_pad
    owned = lax.psum_scatter(
        lax.dot_general(
            columns, d_kv, (((0,), (0,)), ((), ())), preferred_element_type=jnp.float32
        ),
        "fsdp",
        scatter_dimension=0,
        tiled=True,
    )
    d_weight = lax.psum(owned, "dp")
    d_gain = lax.psum(gain_term, ("dp", "fsdp"))
    return (d_weight, d_gain)


def solution(mesh):
    in_specs = (
        P(("dp", "fsdp"), None, None),
        P(("dp", "fsdp"), None, None),
        P(("dp", "fsdp"), None, None),
        P(("dp", "fsdp"), None),
        P(("dp", "fsdp"), None),
        P(("dp", "fsdp"), None),
        P("fsdp", None),
        P(),
        P(),
    )
    out_specs = (P("fsdp", None), P())
    return jax.shard_map(shards, mesh=mesh, in_specs=in_specs, out_specs=out_specs, check_vma=False)
```

profile of v0, /device:TPU:0, one launch (start us, length us, event | category | flops | bytes accessed | tf_op | source)
XLA Modules:
  0.0 176.6 jit_solution(304360685169736255)
XLA Ops:
  7.2 0.0 copy-start
  7.2 0.0 all-gather.2.cloned.1.call-start
  7.2 0.7 all-gather.2.cloned.1.call-update
  7.9 0.0 reduce-scatter.2.cloned.1.call-start
  8.0 0.7 compare_convert_fusion
  8.6 0.3 reduce-window.12
  9.0 0.1 slice.15
  9.1 0.1 slice_reduce_fusion
  9.2 0.1 broadcast_add_fusion
  9.3 2.3 %scatter_custom_fusion = s32[128]{0:T(128)S(1)} fusion(s32[256]{0:T(256)S(1)} %bitcast.85, s32[256]{0:T(256)S(1)} %broadcast.196, s32[]{:T(128)} %constant.50.clone.1), kind=kCustom, calls=%fused_computation.70 | custom fusion | flops 256 | bytes 516 | tf_op jit(solution)/shard_map/scatter-add | solution.py:59
  11.6 0.1 copy.49
  11.7 0.2 select_n.65
  11.9 1.3 fusion.39
  13.2 0.8 fusion.28
  14.0 1.3 gather_fusion.1
  15.3 1.6 gather_fusion
  16.9 1.2 convert_bitcast_fusion.1
  18.1 0.2 copy.72
  18.3 0.0 copy-start.2
  18.3 1.0 copy-done.2
  19.3 0.3 multiply_reduce_fusion
  19.6 0.1 copy.50
  19.7 0.1 copy.51
  19.8 0.0 copy-done.9
  19.8 1.8 multiply_convert_fusion
  21.6 0.0 copy-start.7
  21.6 0.0 copy-start.8
  21.6 0.7 gather_fusion.2
  22.3 0.9 copy.60
  23.2 1.1 convert_bitcast_fusion
  24.4 0.0 copy-start.1
  24.4 0.2 copy.73
  24.6 0.0 copy-done.7
  24.6 0.0 copy-done.8
  24.6 0.3 fusion.15
  25.0 1.4 gather_fusion.3
  26.3 0.7 iota_compare_fusion.2
  27.0 1.2 broadcast_select_fusion
  28.2 0.9 copy.62
  29.1 0.0 copy-done.1
  29.1 0.1 fusion.22
  29.2 0.0 copy-start.6
  29.2 0.0 copy-start.10
  29.2 17.1 %all-gather.2.cloned.1.call-done = bf16[5120,256]{1,0:T(8,128)(2,1)} async-done(((bf16[640,256]{1,0:T(8,128)(2,1)}), bf16[5120,256]{1,0:T(8,128)(2,1)}) %all-gather.2.cloned.1.call-update) | async-done | bytes 2621456 | tf_op jit(solution)/shard_map/all_gather | solution.py:42
  46.3 2.9 %fusion.1 = f32[256,256]{0,1:T(8,128)S(1)} fusion(bf16[5120,256]{1,0:T(8,128)(2,1)} %all-gather.2.cloned.1.call-done, bf16[1,256,5120]{2,1,0:T(8,128)(2,1)S(1)} %copy-done), kind=kOutput, calls=%fused_computation.7 | convolution fusion | flops 671088640 | bytes 5505024 | tf_op jit(solution)/shard_map/dot_general | solution.py:40
  49.2 0.0 copy-done.6
  49.2 0.0 copy-done.10
  49.2 0.5 fusion.40
  49.7 0.2 copy-done.3
  49.9 0.8 copy-done.5
  50.7 0.1 fusion.18
  50.8 1.2 copy.57
  52.0 1.5 fusion.12
  53.5 1.3 fusion.14
  54.8 2.2 %multiply_reduce_fusion.1 = (f32[128]{0:T(128)S(1)}, f32[256]{0:T(256)S(1)}, f32[256,128]{0,1:T(8,128)S(1)}) fusion(f32[256,256]{0,1:T(8,128)} %copy-done.3, f32[256]{0:T(256)S(1)} %add_rsqrt_fusion.1, f32[128]{0:T(128)S(1)} %copy-done.10, bf16[128,8,128]{0,2,1:T(8,128)(2,1)} %copy.60, bf16[128,8,128]{0,2,1:T(8,128)(2,1)} %copy.62, f32[8,128]{1,0:T(8,128)S(1)} %copy.58, ...), kind=kOutput, calls=%fused_computation.41 | convolution fusion | flops 135724672 | bytes 1911808 | tf_op jit(solution)/shard_map/hqk,qhd->kd/dot_general | solution.py:24
  57.0 0.1 multiply_convert_fusion.1
  57.1 3.2 %convolution_bitcast_fusion = f32[5120,256]{0,1:T(8,128)} fusion(bf16[1,256,5120]{2,1,0:T(8,128)(2,1)S(1)} %copy-done, bf16[256,128]{0,1:T(8,128)(2,1)S(1)} %fusion.14, bf16[256,128]{0,1:T(8,128)(2,1)S(1)} %multiply_convert_fusion.1), kind=kOutput, calls=%fused_computation.5 | convolution fusion | flops 671350784 | bytes 7995392 | tf_op jit(solution)/shard_map/dot_general | solution.py:80
  60.2 0.0 reduce-scatter.2.cloned.1.call-update
  60.3 0.0 all-reduce.2.cloned.1.call-start
  60.3 59.0 %reduce-scatter.2.cloned.1.call-done = f32[640,256]{0,1:T(8,128)} async-done(((f32[5120,256]{0,1:T(8,128)}), f32[640,256]{0,1:T(8,128)}) %reduce-scatter.2.cloned.1.call-update) | async-done | bytes 655376 | tf_op jit(solution)/shard_map/reduce_scatter | solution.py:79
  119.3 0.0 all-reduce.2.cloned.1.call-update
  119.3 37.9 %psum.15 = f32[128]{0:T(128)} all-reduce(f32[128]{0:T(128)S(1)} %get-tuple-element.12), channel_id=1, replica_groups=mesh['dp'=4,'fsdp'=8] {'dp','fsdp'}, use_global_device_ids=true, to_apply=%region_14.15 | all-reduce | flops 128 | bytes 1024 | tf_op jit(solution)/shard_map/psum | solution.py:88
  157.2 10.7 %all-reduce.2.cloned.1.call-done = f32[640,256]{0,1:T(8,128)} async-done(((f32[640,256]{0,1:T(8,128)}), f32[640,256]{0,1:T(8,128)}) %all-reduce.2.cloned.1.call-update) | async-done | bytes 655376 | tf_op jit(solution)/shard_map/psum | solution.py:87
  167.9 2.2 %copy.63 = f32[640,256]{1,0:T(8,128)} copy(f32[640,256]{0,1:T(8,128)} %all-reduce.2.cloned.1.call-done) | data formatting | bytes 1310720
  (17 shorter events, 0.2 us)
Async XLA Ops:
  7.2 39.1 %copy-start = (bf16[1,256,5120]{2,1,0:T(8,128)(2,1)S(1)}, bf16[1,256,5120]{2,1,0:T(8,128)(2,1)}, u32[]{:S(2)}) copy-start(bf16[1,256,5120]{2,1,0:T(8,128)(2,1)} %param.9) | copy-start | bytes 7864324
  7.2 39.1 %all-gather.2.cloned.1.call-start = ((), (), s32[]{:S(2)}) async-start(), calls=%async_computation.1 | async-start | bytes 2949120 | tf_op jit(solution)/shard_map/all_gather | solution.py:42
  7.9 111.4 %reduce-scatter.2.cloned.1.call-start = ((), (), s32[]{:S(2)}) async-start(), calls=%async_computation.2 | async-start | bytes 5898240 | tf_op jit(solution)/shard_map/reduce_scatter | solution.py:79
  16.9 2.9 %copy-start.9 = (f32[128]{0:T(128)S(1)}, f32[128]{0:T(128)}, u32[]{:S(2)}) copy-start(f32[128]{0:T(128)} %param.17) | copy-start | bytes 1540
  18.3 1.0 copy-start.2
  21.6 3.0 %copy-start.7 = (s32[1,256]{1,0:T(1,128)S(1)}, s32[1,256]{1,0:T(1,128)}, u32[]{:S(2)}) copy-start(s32[1,256]{1,0:T(1,128)} %param.13) | copy-start | bytes 3076
  21.6 3.0 %copy-start.8 = (f32[1,256]{1,0:T(1,128)S(1)}, f32[1,256]{1,0:T(1,128)}, u32[]{:S(2)}) copy-start(f32[1,256]{1,0:T(1,128)} %param.12) | copy-start | bytes 3076
  24.4 4.7 %copy-start.1 = (s32[1,256]{1,0:T(1,128)S(1)}, s32[1,256]{1,0:T(1,128)}, u32[]{:S(2)}) copy-start(s32[1,256]{1,0:T(1,128)} %param.14) | copy-start | bytes 3076
  29.2 20.0 %copy-start.6 = (bf16[128,8,128]{0,2,1:T(8,128)(2,1)S(1)}, bf16[128,8,128]{0,2,1:T(8,128)(2,1)}, u32[]{:S(2)}) copy-start(bf16[128,8,128]{0,2,1:T(8,128)(2,1)} %copy.60) | copy-start | bytes 786436
  29.2 20.0 %copy-start.10 = (f32[128]{0:T(128)S(1)}, f32[128]{0:T(128)}, u32[]{:S(2)}) copy-start(f32[128]{0:T(128)} %param.16) | copy-start | bytes 1540
  49.1 0.7 copy-start.3
  49.7 1.0 copy-start.5
  54.7 2.2 %copy-start.4 = (f32[256,256]{0,1:T(8,128)S(1)}, f32[256,256]{0,1:T(8,128)}, u32[]{:S(2)}) copy-start(f32[256,256]{0,1:T(8,128)} %copy-done.3) | copy-start | bytes 786436
  60.3 107.7 %all-reduce.2.cloned.1.call-start = ((), (), s32[]{:S(2)}) async-start(), calls=%async_computation.3 | async-start | bytes 1310720 | tf_op jit(solution)/shard_map/psum | solution.py:87
Sparse Core Ops, SparseCore 0:
  9.7 36.5 all-gather.1
  60.4 58.8 reduce-scatter.1
  122.3 45.5 all-reduce.1
where the time goes:
time: 177 us
  waiting for transfers between devices  87.4 us (49%)
  blocking collectives  37.9 us (21%)
  between operations  14 us (8%)
  local copies, waits for them, and re-layouts  13.1 us (7%)
  other arithmetic  12.6 us (7%)
  matrix products  11.4 us (6%)
    reduce_scatter x1, waiting for transfers between devices, shards(): lax.psum_scatter(lax.dot_general(columns, d_kv, (((0,), (0,)), ((), ())),...  59 us
    psum x1, blocking collectives, shards(): d_gain = lax.psum(gain_term, ('dp', 'fsdp'))  37.9 us
    all_gather x1, waiting for transfers between devices, shards(): lax.all_gather(w_kv, 'fsdp', axis=0, tiled=True)  17.1 us
    psum x1, waiting for transfers between devices, shards(): d_weight = lax.psum(owned, 'dp')  10.7 us
    unnamed x25, local copies, waits for them, and re-layouts  4.57 us
  transfers between devices with their start and end apart: 3, of which 3 were waited for; matrix products, arithmetic and copies ran while one was open for 11% of the time, Pallas kernels for 0%

commit v1 on v0

v1 whole, which is shorter than its diff:
```python
import functools
import math

import jax
import jax.numpy as jnp
from jax import lax
from jax.experimental import pallas as pl
from jax.experimental.pallas import tpu as pltpu
from jax.sharding import PartitionSpec as P

CAP = 128
epsilon = 1e-06
MESH = pl.DeviceIdType.MESH
F32 = jnp.float32
BF16 = jnp.bfloat16


def dot_last(a, b):
    return lax.dot_general(a, b, (((1,), (1,)), ((), ())), preferred_element_type=F32)


def dot(a, b):
    return jnp.dot(a, b, preferred_element_type=F32)


def body(
    data,
    owners,
    hidden,
    queries,
    upstream,
    advantage,
    selected,
    segment,
    w_own,
    k_gain,
    q_gain,
    d_weight,
    d_gain,
    hid,
    hid_t,
    w_half,
    q_raw,
    u_raw,
    q_sel,
    c_sel,
    allowed,
    kv_out,
    kv_in,
    d_kv,
    part,
    from_data,
    z_out,
    from_z,
    final,
    gain_core,
    gain_data,
    gain_z,
    local_sem,
    hid_sem,
    w_z_sem,
    w_data_sem,
    core_sem,
    part_sem,
    z_sem,
    final_sem,
    gain_data_sem,
    gain_z_sem,
):
    chips = owners // 2
    rows = w_own.shape[0]
    share = rows // data
    length = hidden.shape[0]
    head_dim = k_gain.shape[1]
    heads = queries.shape[1] // head_dim
    cap = allowed.shape[1] // 2
    scale = head_dim ** (-0.5)
    dp = lax.axis_index("dp")
    me = lax.axis_index("fsdp")
    chip = me // 2
    core = me % 2
    sibling = {"dp": dp, "fsdp": chip * 2 + 1 - core}

    def chip_at(k):
        return lax.rem(chip + k, chips)

    def data_at(k):
        return lax.rem(dp + k, data)

    def to_chip(other):
        return {"dp": dp, "fsdp": other * 2 + core}

    def to_data(other):
        return {"dp": other, "fsdp": me}

    def rows_of(p):
        return pl.ds(pl.multiple_of(p * share, 16), share)

    def remote(src, dst, send, recv, device):
        return pltpu.make_async_remote_copy(
            src_ref=src, dst_ref=dst, send_sem=send, recv_sem=recv, device_id=device, device_id_type=MESH
        )

    own_w = pltpu.make_async_copy(w_own, w_half.at[chip], local_sem.at[0])
    own_w.start()
    load_q = pltpu.make_async_copy(queries, q_raw, local_sem.at[1])
    load_q.start()
    load_u = pltpu.make_async_copy(upstream, u_raw, local_sem.at[2])
    load_u.start()
    loads = []
    for j in range(chips):
        cols = pl.ds(pl.multiple_of((2 * j + core) * rows, 128), rows)
        load = pltpu.make_async_copy(
            hidden.at[:, cols], hid.at[0, :, pl.ds(j * rows, rows)], hid_sem.at[0, j]
        )
        load.start()
        loads.append(load)

    barrier = pltpu.get_barrier_semaphore()
    pl.semaphore_signal(barrier, inc=1, device_id=sibling, device_id_type=MESH)
    for k in range(1, chips):
        pl.semaphore_signal(barrier, inc=1, device_id=to_chip(chip_at(k)), device_id_type=MESH)
    for k in range(1, data):
        pl.semaphore_signal(barrier, inc=1, device_id=to_data(data_at(k)), device_id_type=MESH)
    pl.semaphore_wait(barrier, chips + data - 1)

    mine = rows_of(dp)
    sends = []
    for k in range(1, chips):
        copy = remote(
            w_own.at[mine], w_half.at[chip, mine], w_z_sem.at[0, k], w_z_sem.at[1, k], to_chip(chip_at(k))
        )
        copy.start()
        sends.append(copy)
    swaps = []
    for j in range(chips):
        cols = pl.ds(pl.multiple_of((2 * j + 1 - core) * rows, 128), rows)
        copy = remote(
            hidden.at[:, cols],
            hid.at[1, :, pl.ds(j * rows, rows)],
            hid_sem.at[1, j],
            hid_sem.at[2, j],
            sibling,
        )
        copy.start()
        swaps.append(copy)

    chosen = selected[...].astype(F32)
    places = lax.broadcasted_iota(jnp.int32, (length, length), 0)
    others = lax.broadcasted_iota(jnp.int32, (length, length), 1)
    upto = places <= others
    rank = dot(jnp.broadcast_to(chosen, (16, length)).astype(BF16), upto.astype(F32).astype(BF16))[:1]
    slots = lax.broadcasted_iota(jnp.int32, (cap, length), 0).astype(F32) + 1.0
    pick = jnp.where(rank == slots, chosen, 0.0)
    pick_b = pick.astype(BF16)
    token_weight = jnp.sum(pick * (advantage[...] * chosen), axis=1, keepdims=True)
    groups = jnp.broadcast_to(segment[...].astype(F32), (length, length))
    allowed_full = jnp.where((groups == groups.T) & upto, 1.0, 0.0).astype(BF16)
    allowed_sel = dot_last(allowed_full, pick_b)
    allowed[:, :cap] = allowed_sel
    allowed[:, cap:] = allowed_sel

    def forward(k):
        sends[k - 1].wait_recv()
        source = chip_at(chips - k)
        for d in range(1, data):
            copy = remote(
                w_half.at[source, mine],
                w_half.at[source, mine],
                w_data_sem.at[0, k, d],
                w_data_sem.at[1, k, d],
                to_data(data_at(d)),
            )
            copy.start()
            forwards.append(copy)

    forwards = []
    for k in range(1, chips):
        forward(k)

    load_q.wait()
    load_u.wait()
    for h in range(heads):
        lanes = pl.ds(h * head_dim, head_dim)
        query = dot(pick_b, q_raw[:, lanes])
        query_scale = lax.rsqrt(jnp.mean(query * query, axis=-1, keepdims=True) + epsilon)
        q_sel[pl.ds(h * cap, cap)] = (query * query_scale * q_gain[...]).astype(BF16)
        grad = dot(pick_b, u_raw[:, lanes])
        c_sel[pl.ds(h * cap, cap)] = (token_weight * grad).astype(BF16)

    for j in range(chips):
        loads[j].wait()
        hid_t[pl.ds(j * rows, rows), :length] = hid[0, :, pl.ds(j * rows, rows)].T
    for j in range(chips):
        swaps[j].wait()
        hid_t[pl.ds(j * rows, rows), length:] = hid[1, :, pl.ds(j * rows, rows)].T

    own_w.wait()
    for copy in forwards:
        copy.wait_recv()

    weight = w_half[...].reshape(chips * rows, w_half.shape[2])
    kv_out[...] = dot(hid[1], weight)
    swap_kv = remote(kv_out, kv_in, core_sem.at[0], core_sem.at[1], sibling)
    swap_kv.start()
    key_value = dot(hid[0], weight)
    swap_kv.wait()
    key_value = key_value + kv_in[...]

    k_raw = key_value[:, :head_dim]
    k_scale = lax.rsqrt(jnp.mean(k_raw * k_raw, axis=-1, keepdims=True) + epsilon)
    k_hat = k_raw * k_scale
    k_norm = (k_hat * k_gain[...]).astype(BF16)
    values = key_value[:, head_dim:].astype(BF16)
    d_key = jnp.zeros((length, head_dim), F32)
    d_value = jnp.zeros((length, head_dim), F32)
    for h in range(heads // 2):
        pair = pl.ds(h * 2 * cap, 2 * cap)
        q_pair = q_sel[pair]
        c_pair = c_sel[pair]
        expo = jnp.exp(dot_last(k_norm, q_pair) * scale) * allowed[...]
        total = jnp.sum(expo, axis=0, keepdims=True)
        probs = expo * (1.0 / jnp.where(total > 0.0, total, 1.0))
        probs_b = probs.astype(BF16)
        dprob = dot_last(values, c_pair)
        delta = jnp.sum(probs_b.astype(F32) * dprob, axis=0, keepdims=True)
        dscore = (probs * (dprob - delta) * scale).astype(BF16)
        d_key += dot(dscore, q_pair)
        d_value += dot(probs_b, c_pair)
    d_khat = d_key * k_gain[...]
    d_kraw = k_scale * (d_khat - k_hat * jnp.mean(d_khat * k_hat, axis=-1, keepdims=True))
    d_kv[0, :, :head_dim] = d_kraw.astype(BF16)
    d_kv[0, :, head_dim:] = d_value.astype(BF16)
    swap_d = remote(d_kv.at[0], d_kv.at[1], core_sem.at[2], core_sem.at[3], sibling)
    swap_d.start()
    gain = jnp.sum(d_key * k_hat, axis=0, keepdims=True)
    gain_core[0] = jnp.broadcast_to(gain, (8, head_dim))
    swap_g = remote(gain_core.at[0], gain_core.at[1], core_sem.at[4], core_sem.at[5], sibling)
    swap_g.start()
    swap_d.wait()

    both = d_kv[...].reshape(2 * length, d_kv.shape[2])
    parts = []
    for k in range(1, chips + 1):
        target = chip_at(k)
        block = hid_t[pl.ds(pl.multiple_of(target * rows, 128), rows), :]
        part[target] = dot(block, both).astype(BF16)
        for d in range(1, data):
            other = data_at(d)
            copy = remote(
                part.at[target, rows_of(other)],
                from_data.at[d, target],
                part_sem.at[0, k - 1, d],
                part_sem.at[1, k - 1, d],
                to_data(other),
            )
            copy.start()
            parts.append(copy)
    swap_g.wait()
    gain_data[dp] = gain_core[0] + gain_core[1]
    gains = []
    for d in range(1, data):
        copy = remote(
            gain_data.at[dp], gain_data.at[dp], gain_data_sem.at[0, d], gain_data_sem.at[1, d], to_data(data_at(d))
        )
        copy.start()
        gains.append(copy)

    columns = []
    for k in range(1, chips + 1):
        target = chip_at(k)
        for d in range(1, data):
            parts[(k - 1) * (data - 1) + d - 1].wait_recv()
        summed = part[target, rows_of(dp)].astype(F32)
        for d in range(1, data):
            summed += from_data[d, target].astype(F32)
        if k < chips:
            z_out[k] = summed.astype(BF16)
            copy = remote(z_out.at[k], from_z.at[k], z_sem.at[0, k], z_sem.at[1, k], to_chip(target))
            copy.start()
            columns.append(copy)

    for copy in gains:
        copy.wait()
    gain_sum = gain_data[0]
    for d in range(1, data):
        gain_sum += gain_data[d]
    gain_z[chip] = gain_sum
    z_gains = []
    for k in range(1, chips):
        copy = remote(
            gain_z.at[chip], gain_z.at[chip], gain_z_sem.at[0, k], gain_z_sem.at[1, k], to_chip(chip_at(k))
        )
        copy.start()
        z_gains.append(copy)

    for k in range(1, chips):
        columns[k - 1].wait_recv()
        summed += from_z[k].astype(F32)
    final[mine] = summed.astype(BF16)
    finals = []
    for d in range(1, data):
        copy = remote(final.at[mine], final.at[mine], final_sem.at[0, d], final_sem.at[1, d], to_data(data_at(d)))
        copy.start()
        finals.append(copy)

    for copy in z_gains:
        copy.wait()
    gain_sum = gain_z[0]
    for k in range(1, chips):
        gain_sum += gain_z[k]
    d_gain[...] = gain_sum

    for copy in sends + forwards + parts + columns:
        copy.wait_send()
    for copy in finals:
        copy.wait()
    d_weight[...] = final[...].astype(F32)


def shards(data, owners, hidden, queries, upstream, advantage, selected, segment, w_kv, k_gain, q_gain):
    hidden_row = hidden[0]
    length, width = hidden_row.shape
    rows_dev, columns = w_kv.shape
    head_dim = k_gain.shape[0]
    heads = queries.shape[2] // head_dim
    unit = math.lcm(128, 16 * data)
    rows = -(-rows_dev // unit) * unit
    chips = owners // 2
    share = rows // data
    if rows_dev * owners != width:
        hidden_row = jnp.pad(hidden_row, ((0, 0), (0, rows_dev * owners - width)))
    if rows != rows_dev:
        blocks = hidden_row.reshape(length, owners, rows_dev)
        hidden_row = jnp.pad(blocks, ((0, 0), (0, 0), (0, rows - rows_dev))).reshape(length, owners * rows)
        w_kv = jnp.pad(w_kv, ((0, rows - rows_dev), (0, 0)))
    vmem = pl.BlockSpec(memory_space=pltpu.VMEM)
    hbm = pl.BlockSpec(memory_space=pl.ANY)
    dma = pltpu.SemaphoreType.DMA
    d_weight, d_gain = pl.pallas_call(
        functools.partial(body, data, owners),
        out_shape=(
            jax.ShapeDtypeStruct((rows, columns), F32),
            jax.ShapeDtypeStruct((8, head_dim), F32),
        ),
        in_specs=[hbm, hbm, hbm, vmem, vmem, vmem, hbm, vmem, vmem],
        out_specs=(vmem, vmem),
        scratch_shapes=[
            pltpu.VMEM((2, length, chips * rows), BF16),
            pltpu.VMEM((chips * rows, 2 * length), BF16),
            pltpu.VMEM((chips, rows, columns), BF16),
            pltpu.VMEM((length, heads * head_dim), BF16),
            pltpu.VMEM((length, heads * head_dim), BF16),
            pltpu.VMEM((heads * CAP, head_dim), BF16),
            pltpu.VMEM((heads * CAP, head_dim), BF16),
            pltpu.VMEM((length, 2 * CAP), F32),
            pltpu.VMEM((length, columns), F32),
            pltpu.VMEM((length, columns), F32),
            pltpu.VMEM((2, length, columns), BF16),
            pltpu.VMEM((chips, rows, columns), BF16),
            pltpu.VMEM((data, chips, share, columns), BF16),
            pltpu.VMEM((chips, share, columns), BF16),
            pltpu.VMEM((chips, share, columns), BF16),
            pltpu.VMEM((rows, columns), BF16),
            pltpu.VMEM((2, 8, head_dim), F32),
            pltpu.VMEM((data, 8, head_dim), F32),
            pltpu.VMEM((chips, 8, head_dim), F32),
            dma((3,)),
            dma((3, chips)),
            dma((2, chips)),
            dma((2, chips, data)),
            dma((6,)),
            dma((2, chips, data)),
            dma((2, chips)),
            dma((2, data)),
            dma((2, data)),
            dma((2, chips)),
        ],
        compiler_params=pltpu.CompilerParams(
            collective_id=0, has_side_effects=True, vmem_limit_bytes=52 * 1024 * 1024
        ),
        cost_estimate=pl.CostEstimate(flops=2_000_000_000, bytes_accessed=6_000_000, transcendentals=300_000),
        name="kv_backward",
    )(
        hidden_row,
        queries[0],
        upstream[0],
        advantage,
        selected,
        segment,
        w_kv,
        k_gain.reshape(1, head_dim),
        q_gain.reshape(1, head_dim),
    )
    return (d_weight[:rows_dev], d_gain[0])


def solution(mesh):
    in_specs = (
        P(("dp", "fsdp"), None, None),
        P(("dp", "fsdp"), None, None),
        P(("dp", "fsdp"), None, None),
        P(("dp", "fsdp"), None),
        P(("dp", "fsdp"), None),
        P(("dp", "fsdp"), None),
        P("fsdp", None),
        P(),
        P(),
    )
    out_specs = (P("fsdp", None), P())
    return jax.shard_map(
        functools.partial(shards, mesh.shape["dp"], mesh.shape["fsdp"]),
        mesh=mesh,
        in_specs=in_specs,
        out_specs=out_specs,
        check_vma=False,
    )
```

time: 177 us -> 61.1 us (0.35)
  waiting for transfers between devices: 87.4 us -> 0 us
  Pallas kernels: 0 us -> 51.2 us
  blocking collectives: 37.9 us -> 0 us
  between operations: 14 us -> 0.66 us
  other arithmetic: 12.6 us -> 0 us
  matrix products: 11.4 us -> 0 us
  local copies, waits for them, and re-layouts: 13.1 us -> 8.87 us
    reduce_scatter x1 -> x0, waiting for transfers between devices: 59 us -> none  [shards(): lax.psum_scatter(lax.dot_general(columns, d_kv, (((0,), (0,)), ((), ())),...]
    pallas_call x0 -> x1, Pallas kernels: none -> 51.2 us  [shards(): pl.pallas_call(functools.partial(body, data, owners), out_shape=(jax.Shap...]
    psum x1 -> x0, blocking collectives: 37.9 us -> none  [shards(): d_gain = lax.psum(gain_term, ('dp', 'fsdp'))]
    all_gather x1 -> x0, waiting for transfers between devices: 17.1 us -> none  [shards(): lax.all_gather(w_kv, 'fsdp', axis=0, tiled=True)]
    dot_general x6 -> x0, matrix products: 11.4 us -> none  [the longest x1 3.17 us: shards(): lax.dot_general(columns, d_kv, (((0,), (0,)), ((), ())), preferred_elemen...]
    psum x1 -> x0, waiting for transfers between devices: 10.7 us -> none  [shards(): d_weight = lax.psum(owned, 'dp')]
    gather x5 -> x0, local copies, waits for them, and re-layouts: 5.87 us -> none  [the longest x1 1.64 us: shards(): segment_row[picked]]
    unnamed x25 -> x17, local copies, waits for them, and re-layouts: 4.57 us -> 8.36 us
  transfers between devices with their start and end apart: 3 -> 0, of which waited for: 3 -> 0; matrix products, arithmetic and copies ran while one was open for 11% -> 0% of each run, Pallas kernels for 0% -> 0%
where the time goes in v1:
time: 61.1 us; the launch traced here: 60.8 us
  Pallas kernels  51.2 us (84%)
  local copies, waits for them, and re-layouts  8.87 us (15%)
  between operations  0.66 us (1%)
    pallas_call x1, Pallas kernels, shards(): pl.pallas_call(functools.partial(body, data, owners), out_shape=(jax.Shap...  51.2 us
    unnamed x17, local copies, waits for them, and re-layouts  8.36 us

profile of v1, /device:TPU:0, one launch (start us, length us, event | category | flops | bytes accessed | tf_op | source)
XLA Modules:
  0.0 60.8 jit_solution(10355548313479079489)
XLA Ops:
  0.6 0.0 copy-start
  0.6 1.0 %copy-done = bf16[1,256,1024]{2,1,0:T(8,128)(2,1)S(1)} copy-done((bf16[1,256,1024]{2,1,0:T(8,128)(2,1)S(1)}, bf16[1,256,1024]{2,1,0:T(8,128)(2,1)}, u32[]{:S(2)}) %copy-start) | copy-done | bytes 524312
  1.7 0.0 copy-start.1
  1.7 1.0 %copy-done.1 = bf16[1,256,1024]{2,1,0:T(8,128)(2,1)S(1)} copy-done((bf16[1,256,1024]{2,1,0:T(8,128)(2,1)S(1)}, bf16[1,256,1024]{2,1,0:T(8,128)(2,1)}, u32[]{:S(2)}) %copy-start.1) | copy-done | bytes 524312
  2.7 0.0 copy-start.2
  2.7 1.0 %copy-done.2 = bf16[640,256]{1,0:T(8,128)(2,1)S(1)} copy-done((bf16[640,256]{1,0:T(8,128)(2,1)S(1)}, bf16[640,256]{1,0:T(8,128)(2,1)}, u32[]{:S(2)}) %copy-start.2) | copy-done | bytes 327704
  3.7 0.0 copy-start.3
  3.7 0.7 %copy-done.3 = f32[1,256]{1,0:T(1,128)S(1)} copy-done((f32[1,256]{1,0:T(1,128)S(1)}, f32[1,256]{1,0:T(1,128)}, u32[]{:S(2)}) %copy-start.3) | copy-done | bytes 1048
  4.4 0.0 copy-start.4
  4.4 0.7 %copy-done.4 = s32[1,256]{1,0:T(1,128)S(1)} copy-done((s32[1,256]{1,0:T(1,128)S(1)}, s32[1,256]{1,0:T(1,128)}, u32[]{:S(2)}) %copy-start.4) | copy-done | bytes 1048
  5.0 0.0 copy-start.5
  5.1 0.7 %copy-done.5 = s32[1,256]{1,0:T(1,128)S(1)} copy-done((s32[1,256]{1,0:T(1,128)S(1)}, s32[1,256]{1,0:T(1,128)}, u32[]{:S(2)}) %copy-start.5) | copy-done | bytes 1048
  5.7 0.0 copy-start.6
  5.7 0.7 %copy-done.6 = f32[128]{0:T(128)S(1)} copy-done((f32[128]{0:T(128)S(1)}, f32[128]{0:T(128)}, u32[]{:S(2)}) %copy-start.6) | copy-done | bytes 536
  6.4 0.0 copy-start.7
  6.4 0.7 %copy-done.7 = f32[128]{0:T(128)S(1)} copy-done((f32[128]{0:T(128)S(1)}, f32[128]{0:T(128)}, u32[]{:S(2)}) %copy-start.7) | copy-done | bytes 536
  7.0 51.2 %kv_backward.1 = (f32[640,256]{1,0:T(8,128)}, f32[8,128]{1,0:T(8,128)S(1)}) custom-call(bf16[256,5120]{1,0:T(8,128)(2,1)} %bitcast.11, bf16[256,1024]{1,0:T(8,128)(2,1)S(1)} %bitcast.7, bf16[256,1024]{1,0:T(8,128)(2,1)S(1)} %bitcast.8, f32[1,256]{1,0:T(1,128)S(1)} %copy-done.3, s32[1,256]{1,0:T(1,128)S(1)} %copy-done.4, s32[1,256]{1,0:T(1,128)S(1)} %copy-done.5, ...), custom_call_target="tpu_custom_call" | custom-call | flops 2000000000 | bytes 6000000 | tf_op jit(solution)/shard_map/kv_backward/pallas_call | solution.py:340
  58.3 0.5 slice_bitcast_fusion
  58.8 2.0 %copy.12 = f32[640,256]{1,0:T(8,128)} copy(f32[640,256]{1,0:T(8,128)} %get-tuple-element.8) | data formatting | bytes 1310720
Async XLA Ops:
  0.6 1.0 %copy-start = (bf16[1,256,1024]{2,1,0:T(8,128)(2,1)S(1)}, bf16[1,256,1024]{2,1,0:T(8,128)(2,1)}, u32[]{:S(2)}) copy-start(bf16[1,256,1024]{2,1,0:T(8,128)(2,1)} %param.10) | copy-start | bytes 1572868
  1.7 1.0 %copy-start.1 = (bf16[1,256,1024]{2,1,0:T(8,128)(2,1)S(1)}, bf16[1,256,1024]{2,1,0:T(8,128)(2,1)}, u32[]{:S(2)}) copy-start(bf16[1,256,1024]{2,1,0:T(8,128)(2,1)} %param.11) | copy-start | bytes 1572868
  2.7 1.0 %copy-start.2 = (bf16[640,256]{1,0:T(8,128)(2,1)S(1)}, bf16[640,256]{1,0:T(8,128)(2,1)}, u32[]{:S(2)}) copy-start(bf16[640,256]{1,0:T(8,128)(2,1)} %w_own.1) | copy-start | bytes 983044
  3.7 0.7 %copy-start.3 = (f32[1,256]{1,0:T(1,128)S(1)}, f32[1,256]{1,0:T(1,128)}, u32[]{:S(2)}) copy-start(f32[1,256]{1,0:T(1,128)} %advantage.1) | copy-start | bytes 3076
  4.4 0.7 %copy-start.4 = (s32[1,256]{1,0:T(1,128)S(1)}, s32[1,256]{1,0:T(1,128)}, u32[]{:S(2)}) copy-start(s32[1,256]{1,0:T(1,128)} %selected.1) | copy-start | bytes 3076
  5.0 0.7 %copy-start.5 = (s32[1,256]{1,0:T(1,128)S(1)}, s32[1,256]{1,0:T(1,128)}, u32[]{:S(2)}) copy-start(s32[1,256]{1,0:T(1,128)} %segment.1) | copy-start | bytes 3076
  5.7 0.7 %copy-start.6 = (f32[128]{0:T(128)S(1)}, f32[128]{0:T(128)}, u32[]{:S(2)}) copy-start(f32[128]{0:T(128)} %param.16) | copy-start | bytes 1540
  6.4 0.7 %copy-start.7 = (f32[128]{0:T(128)S(1)}, f32[128]{0:T(128)}, u32[]{:S(2)}) copy-start(f32[128]{0:T(128)} %param.17) | copy-start | bytes 1540

commit v2 on v1

--- a/solution.py
+++ b/solution.py
@@ -24,7 +24,7 @@
 
 
 def body(
-    data,
+    grid,
     owners,
     hidden,
     queries,
@@ -37,6 +37,11 @@
     q_gain,
     d_weight,
     d_gain,
+    adv_in,
+    sel_in,
+    seg_in,
+    kg_in,
+    qg_in,
     hid,
     hid_t,
     w_half,
@@ -46,10 +51,16 @@
     c_sel,
     allowed,
     kv_out,
+    kv_own,
     kv_in,
     d_kv,
     part,
-    from_data,
+    mid_row,
+    mid_col,
+    relay_row,
+    relay_col,
+    from_row,
+    from_col,
     z_out,
     from_z,
     final,
@@ -59,19 +70,29 @@
     local_sem,
     hid_sem,
     w_z_sem,
-    w_data_sem,
+    w_row_sem,
+    w_col_sem,
+    w_diag_row_sem,
+    w_diag_col_sem,
     core_sem,
-    part_sem,
+    mid_row_sem,
+    mid_col_sem,
+    row_sem,
+    col_sem,
     z_sem,
     final_sem,
     gain_data_sem,
     gain_z_sem,
 ):
+    tall, wide = grid
+    data = tall * wide
     chips = owners // 2
     rows = w_own.shape[0]
     share = rows // data
     length = hidden.shape[0]
     head_dim = k_gain.shape[1]
+    half = w_own.shape[1] // 2
+    low, high = pl.ds(0, half), pl.ds(half, half)
     heads = queries.shape[1] // head_dim
     cap = allowed.shape[1] // 2
     scale = head_dim ** (-0.5)
@@ -87,6 +108,11 @@
     def data_at(k):
         return lax.rem(dp + k, data)
 
+    row, col = dp // wide, dp % wide
+
+    def place(s, t):
+        return lax.rem(row + s, tall) * wide + lax.rem(col + t, wide)
+
     def to_chip(other):
         return {"dp": dp, "fsdp": other * 2 + core}
 
@@ -107,6 +133,13 @@
     load_q.start()
     load_u = pltpu.make_async_copy(upstream, u_raw, local_sem.at[2])
     load_u.start()
+    smalls = []
+    for n, (src, dst) in enumerate(
+        ((advantage, adv_in), (selected, sel_in), (segment, seg_in), (k_gain, kg_in), (q_gain, qg_in))
+    ):
+        load = pltpu.make_async_copy(src, dst, local_sem.at[3 + n])
+        load.start()
+        smalls.append(load)
     loads = []
     for j in range(chips):
         cols = pl.ds(pl.multiple_of((2 * j + core) * rows, 128), rows)
@@ -145,7 +178,9 @@
         copy.start()
         swaps.append(copy)
 
-    chosen = selected[...].astype(F32)
+    for load in smalls:
+        load.wait()
+    chosen = sel_in[...].astype(F32)
     places = lax.broadcasted_iota(jnp.int32, (length, length), 0)
     others = lax.broadcasted_iota(jnp.int32, (length, length), 1)
     upto = places <= others
@@ -153,30 +188,65 @@
     slots = lax.broadcasted_iota(jnp.int32, (cap, length), 0).astype(F32) + 1.0
     pick = jnp.where(rank == slots, chosen, 0.0)
     pick_b = pick.astype(BF16)
-    token_weight = jnp.sum(pick * (advantage[...] * chosen), axis=1, keepdims=True)
-    groups = jnp.broadcast_to(segment[...].astype(F32), (length, length))
+    token_weight = jnp.sum(pick * (adv_in[...] * chosen), axis=1, keepdims=True)
+    groups = jnp.broadcast_to(seg_in[...].astype(F32), (length, length))
     allowed_full = jnp.where((groups == groups.T) & upto, 1.0, 0.0).astype(BF16)
     allowed_sel = dot_last(allowed_full, pick_b)
     allowed[:, :cap] = allowed_sel
     allowed[:, cap:] = allowed_sel
 
+    ahead = []
+    near = {}
+    diag = {}
+
     def forward(k):
         sends[k - 1].wait_recv()
         source = chip_at(chips - k)
-        for d in range(1, data):
-            copy = remote(
+        for t in range(1, wide):
+            near[k, 0, t] = remote(
                 w_half.at[source, mine],
                 w_half.at[source, mine],
-                w_data_sem.at[0, k, d],
-                w_data_sem.at[1, k, d],
-                to_data(data_at(d)),
+                w_row_sem.at[0, k, t - 1],
+                w_row_sem.at[1, k, t - 1],
+                to_data(place(0, t)),
             )
+        for s in range(1, tall):
+            near[k, s, 0] = remote(
+                w_half.at[source, mine],
+                w_half.at[source, mine],
+                w_col_sem.at[0, k, s - 1],
+                w_col_sem.at[1, k, s - 1],
+                to_data(place(s, 0)),
+            )
+        for copy in [near[key] for key in near if key[0] == k]:
             copy.start()
-            forwards.append(copy)
-
-    forwards = []
+            ahead.append(copy)
+
+    def forward_diag(k):
+        source = chip_at(chips - k)
+        for t in range(1, wide):
+            near[k, 0, t].wait_recv()
+            block = w_half.at[source, rows_of(place(0, wide - t)), low]
+            for s in range(1, tall):
+                diag[k, 0, s, t] = remote(
+                    block, block, w_diag_row_sem.at[0, k, s - 1, t - 1], w_diag_row_sem.at[1, k, s - 1, t - 1], to_data(place(s, 0))
+                )
+                diag[k, 0, s, t].start()
+                ahead.append(diag[k, 0, s, t])
+        for s in range(1, tall):
+            near[k, s, 0].wait_recv()
+            block = w_half.at[source, rows_of(place(tall - s, 0)), high]
+            for t in range(1, wide):
+                diag[k, 1, s, t] = remote(
+                    block, block, w_diag_col_sem.at[0, k, s - 1, t - 1], w_diag_col_sem.at[1, k, s - 1, t - 1], to_data(place(0, t))
+                )
+                diag[k, 1, s, t].start()
+                ahead.append(diag[k, 1, s, t])
+
     for k in range(1, chips):
         forward(k)
+        if k > 1:
+            forward_diag(k - 1)
 
     load_q.wait()
     load_u.wait()
@@ -184,10 +254,12 @@
         lanes = pl.ds(h * head_dim, head_dim)
         query = dot(pick_b, q_raw[:, lanes])
         query_scale = lax.rsqrt(jnp.mean(query * query, axis=-1, keepdims=True) + epsilon)
-        q_sel[pl.ds(h * cap, cap)] = (query * query_scale * q_gain[...]).astype(BF16)
+        q_sel[pl.ds(h * cap, cap)] = (query * query_scale * qg_in[...]).astype(BF16)
         grad = dot(pick_b, u_raw[:, lanes])
         c_sel[pl.ds(h * cap, cap)] = (token_weight * grad).astype(BF16)
 
+    if chips > 1:
+        forward_diag(chips - 1)
     for j in range(chips):
         loads[j].wait()
         hid_t[pl.ds(j * rows, rows), :length] = hid[0, :, pl.ds(j * rows, rows)].T
@@ -196,21 +268,33 @@
         hid_t[pl.ds(j * rows, rows), length:] = hid[1, :, pl.ds(j * rows, rows)].T
 
     own_w.wait()
-    for copy in forwards:
-        copy.wait_recv()
-
-    weight = w_half[...].reshape(chips * rows, w_half.shape[2])
-    kv_out[...] = dot(hid[1], weight)
+    for k in range(chips):
+        source = chip_at(chips - k)
+        for key in diag:
+            if key[0] == k:
+                diag[key].wait_recv()
+        cols = pl.ds(pl.multiple_of(source * rows, 128), rows)
+        weight = w_half[source]
+        if k == 0:
+            kv_out[...] = dot(hid[1, :, cols], weight)
+            kv_own[...] = dot(hid[0, :, cols], weight)
+        elif k < chips - 1:
+            kv_out[...] += dot(hid[1, :, cols], weight)
+            kv_own[...] += dot(hid[0, :, cols], weight)
+        else:
+            kv_out[...] += dot(hid[1, :, cols], weight)
     swap_kv = remote(kv_out, kv_in, core_sem.at[0], core_sem.at[1], sibling)
     swap_kv.start()
-    key_value = dot(hid[0], weight)
+    key_value = kv_own[...]
+    if chips > 1:
+        key_value += dot(hid[0, :, cols], weight)
     swap_kv.wait()
     key_value = key_value + kv_in[...]
 
     k_raw = key_value[:, :head_dim]
     k_scale = lax.rsqrt(jnp.mean(k_raw * k_raw, axis=-1, keepdims=True) + epsilon)
     k_hat = k_raw * k_scale
-    k_norm = (k_hat * k_gain[...]).astype(BF16)
+    k_norm = (k_hat * kg_in[...]).astype(BF16)
     values = key_value[:, head_dim:].astype(BF16)
     d_key = jnp.zeros((length, head_dim), F32)
     d_value = jnp.zeros((length, head_dim), F32)
@@ -227,7 +311,7 @@
         dscore = (probs * (dprob - delta) * scale).astype(BF16)
         d_key += dot(dscore, q_pair)
         d_value += dot(probs_b, c_pair)
-    d_khat = d_key * k_gain[...]
+    d_khat = d_key * kg_in[...]
     d_kraw = k_scale * (d_khat - k_hat * jnp.mean(d_khat * k_hat, axis=-1, keepdims=True))
     d_kv[0, :, :head_dim] = d_kraw.astype(BF16)
     d_kv[0, :, head_dim:] = d_value.astype(BF16)
@@ -237,48 +321,134 @@
     gain_core[0] = jnp.broadcast_to(gain, (8, head_dim))
     swap_g = remote(gain_core.at[0], gain_core.at[1], core_sem.at[4], core_sem.at[5], sibling)
     swap_g.start()
-    swap_d.wait()
-
-    both = d_kv[...].reshape(2 * length, d_kv.shape[2])
     parts = []
-    for k in range(1, chips + 1):
+    mids = {}
+    nears = {}
+    columns = []
+    gains = []
+
+    def begin(copy):
+        copy.start()
+        parts.append(copy)
+        return copy
+
+    def make(k):
         target = chip_at(k)
-        block = hid_t[pl.ds(pl.multiple_of(target * rows, 128), rows), :]
-        part[target] = dot(block, both).astype(BF16)
-        for d in range(1, data):
-            other = data_at(d)
-            copy = remote(
-                part.at[target, rows_of(other)],
-                from_data.at[d, target],
-                part_sem.at[0, k - 1, d],
-                part_sem.at[1, k - 1, d],
-                to_data(other),
+        block = pl.ds(pl.multiple_of(target * rows, 128), rows)
+        if k == 1:
+            mixed = dot(hid_t[block, :length], d_kv[0])
+            swap_d.wait()
+            part[target] = (mixed + dot(hid_t[block, length:], d_kv[1])).astype(BF16)
+        else:
+            part[target] = dot(hid_t[block, :], d_kv[...].reshape(2 * length, 2 * half)).astype(BF16)
+        for s in range(1, tall):
+            for t in range(1, wide):
+                share_of = rows_of(place(s, t))
+                mids[k, 0, s, t] = begin(
+                    remote(
+                        part.at[target, share_of, low],
+                        mid_row.at[k - 1, s, t],
+                        mid_row_sem.at[0, k - 1, s - 1, t - 1],
+                        mid_row_sem.at[1, k - 1, s - 1, t - 1],
+                        to_data(place(0, t)),
+                    )
+                )
+                mids[k, 1, s, t] = begin(
+                    remote(
+                        part.at[target, share_of, high],
+                        mid_col.at[k - 1, s, t],
+                        mid_col_sem.at[0, k - 1, s - 1, t - 1],
+                        mid_col_sem.at[1, k - 1, s - 1, t - 1],
+                        to_data(place(s, 0)),
+                    )
+                )
+        for t in range(1, wide):
+            nears[k, 0, t, 0] = begin(
+                remote(
+                    part.at[target, rows_of(place(0, t)), low],
+                    from_row.at[t, k - 1, :, low],
+                    row_sem.at[0, 0, k - 1, t - 1],
+                    row_sem.at[1, 0, k - 1, t - 1],
+                    to_data(place(0, t)),
+                )
             )
-            copy.start()
-            parts.append(copy)
-    swap_g.wait()
-    gain_data[dp] = gain_core[0] + gain_core[1]
-    gains = []
-    for d in range(1, data):
-        copy = remote(
-            gain_data.at[dp], gain_data.at[dp], gain_data_sem.at[0, d], gain_data_sem.at[1, d], to_data(data_at(d))
-        )
-        copy.start()
-        gains.append(copy)
-
-    columns = []
-    for k in range(1, chips + 1):
+        for s in range(1, tall):
+            nears[k, s, 0, 1] = begin(
+                remote(
+                    part.at[target, rows_of(place(s, 0)), high],
+                    from_col.at[s, k - 1, :, high],
+                    col_sem.at[0, 0, k - 1, s - 1],
+                    col_sem.at[1, 0, k - 1, s - 1],
+                    to_data(place(s, 0)),
+                )
+            )
+
+    def relay(k):
         target = chip_at(k)
-        for d in range(1, data):
-            parts[(k - 1) * (data - 1) + d - 1].wait_recv()
-        summed = part[target, rows_of(dp)].astype(F32)
-        for d in range(1, data):
-            summed += from_data[d, target].astype(F32)
+        for s in range(1, tall):
+            sent = part[target, rows_of(place(s, 0)), low].astype(F32)
+            for t in range(1, wide):
+                mids[k, 0, s, t].wait_recv()
+                sent += mid_row[k - 1, s, t].astype(F32)
+            relay_col[k - 1, s] = sent.astype(BF16)
+            nears[k, s, 0, 0] = begin(
+                remote(
+                    relay_col.at[k - 1, s],
+                    from_col.at[s, k - 1, :, low],
+                    col_sem.at[0, 1, k - 1, s - 1],
+                    col_sem.at[1, 1, k - 1, s - 1],
+                    to_data(place(s, 0)),
+                )
+            )
+        for t in range(1, wide):
+            sent = part[target, rows_of(place(0, t)), high].astype(F32)
+            for s in range(1, tall):
+                mids[k, 1, s, t].wait_recv()
+                sent += mid_col[k - 1, s, t].astype(F32)
+            relay_row[k - 1, t] = sent.astype(BF16)
+            nears[k, 0, t, 1] = begin(
+                remote(
+                    relay_row.at[k - 1, t],
+                    from_row.at[t, k - 1, :, high],
+                    row_sem.at[0, 1, k - 1, t - 1],
+                    row_sem.at[1, 1, k - 1, t - 1],
+                    to_data(place(0, t)),
+                )
+            )
+
+    def collect(k):
+        target = chip_at(k)
+        for key in nears:
+            if key[0] == k:
+                nears[key].wait_recv()
+        total = part[target, mine].astype(F32)
+        for s in range(1, tall):
+            total += from_col[s, k - 1].astype(F32)
+        for t in range(1, wide):
+            total += from_row[t, k - 1].astype(F32)
         if k < chips:
-            z_out[k] = summed.astype(BF16)
+            z_out[k] = total.astype(BF16)
             copy = remote(z_out.at[k], from_z.at[k], z_sem.at[0, k], z_sem.at[1, k], to_chip(target))
             copy.start()
             columns.append(copy)
+        return total
+
+    for k in range(1, chips + 3):
+        if k <= chips:
+            make(k)
+        if k == 1:
+            swap_g.wait()
+            gain_data[dp] = gain_core[0] + gain_core[1]
+            for d in range(1, data):
+                copy = remote(
+                    gain_data.at[dp], gain_data.at[dp], gain_data_sem.at[0, d], gain_data_sem.at[1, d], to_data(data_at(d))
+                )
+                copy.start()
+                gains.append(copy)
+        if 1 <= k - 1 <= chips:
+            relay(k - 1)
+        if 1 <= k - 2 <= chips:
+            summed = collect(k - 2)
 
     for copy in gains:
         copy.wait()
@@ -311,19 +481,21 @@
         gain_sum += gain_z[k]
     d_gain[...] = gain_sum
 
-    for copy in sends + forwards + parts + columns:
+    for copy in sends + ahead + parts + columns:
         copy.wait_send()
     for copy in finals:
         copy.wait()
-    d_weight[...] = final[...].astype(F32)
-
-
-def shards(data, owners, hidden, queries, upstream, advantage, selected, segment, w_kv, k_gain, q_gain):
+    d_weight[...] = final[...]
+
+
+def shards(grid, owners, hidden, queries, upstream, advantage, selected, segment, w_kv, k_gain, q_gain):
     hidden_row = hidden[0]
     length, width = hidden_row.shape
     rows_dev, columns = w_kv.shape
     head_dim = k_gain.shape[0]
     heads = queries.shape[2] // head_dim
+    tall, wide = grid
+    data = tall * wide
     unit = math.lcm(128, 16 * data)
     rows = -(-rows_dev // unit) * unit
     chips = owners // 2
@@ -335,17 +507,22 @@
         hidden_row = jnp.pad(blocks, ((0, 0), (0, 0), (0, rows - rows_dev))).reshape(length, owners * rows)
         w_kv = jnp.pad(w_kv, ((0, rows - rows_dev), (0, 0)))
     vmem = pl.BlockSpec(memory_space=pltpu.VMEM)
-    hbm = pl.BlockSpec(memory_space=pl.ANY)
+    hbm = pl.BlockSpec(memory_space=pltpu.HBM)
     dma = pltpu.SemaphoreType.DMA
     d_weight, d_gain = pl.pallas_call(
-        functools.partial(body, data, owners),
+        functools.partial(body, grid, owners),
         out_shape=(
-            jax.ShapeDtypeStruct((rows, columns), F32),
+            jax.ShapeDtypeStruct((rows, columns), BF16),
             jax.ShapeDtypeStruct((8, head_dim), F32),
         ),
-        in_specs=[hbm, hbm, hbm, vmem, vmem, vmem, hbm, vmem, vmem],
+        in_specs=[hbm] * 9,
         out_specs=(vmem, vmem),
         scratch_shapes=[
+            pltpu.VMEM((1, length), F32),
+            pltpu.VMEM((1, length), jnp.int32),
+            pltpu.VMEM((1, length), jnp.int32),
+            pltpu.VMEM((1, head_dim), F32),
+            pltpu.VMEM((1, head_dim), F32),
             pltpu.VMEM((2, length, chips * rows), BF16),
             pltpu.VMEM((chips * rows, 2 * length), BF16),
             pltpu.VMEM((chips, rows, columns), BF16),
@@ -356,28 +533,40 @@
             pltpu.VMEM((length, 2 * CAP), F32),
             pltpu.VMEM((length, columns), F32),
             pltpu.VMEM((length, columns), F32),
+            pltpu.VMEM((length, columns), F32),
             pltpu.VMEM((2, length, columns), BF16),
             pltpu.VMEM((chips, rows, columns), BF16),
-            pltpu.VMEM((data, chips, share, columns), BF16),
+            pltpu.VMEM((chips, tall, wide, share, columns // 2), BF16),
+            pltpu.VMEM((chips, tall, wide, share, columns // 2), BF16),
+            pltpu.VMEM((chips, wide, share, columns // 2), BF16),
+            pltpu.VMEM((chips, tall, share, columns // 2), BF16),
+            pltpu.VMEM((wide, chips, share, columns), BF16),
+            pltpu.VMEM((tall, chips, share, columns), BF16),
             pltpu.VMEM((chips, share, columns), BF16),
             pltpu.VMEM((chips, share, columns), BF16),
             pltpu.VMEM((rows, columns), BF16),
             pltpu.VMEM((2, 8, head_dim), F32),
             pltpu.VMEM((data, 8, head_dim), F32),
             pltpu.VMEM((chips, 8, head_dim), F32),
-            dma((3,)),
+            dma((8,)),
             dma((3, chips)),
             dma((2, chips)),
-            dma((2, chips, data)),
+            dma((2, chips, max(wide - 1, 1))),
+            dma((2, chips, max(tall - 1, 1))),
+            dma((2, chips, max(tall - 1, 1), max(wide - 1, 1))),
+            dma((2, chips, max(tall - 1, 1), max(wide - 1, 1))),
             dma((6,)),
-            dma((2, chips, data)),
+            dma((2, chips, max(tall - 1, 1), max(wide - 1, 1))),
+            dma((2, chips, max(tall - 1, 1), max(wide - 1, 1))),
+            dma((2, 2, chips, max(wide - 1, 1))),
+            dma((2, 2, chips, max(tall - 1, 1))),
             dma((2, chips)),
             dma((2, data)),
             dma((2, data)),
             dma((2, chips)),
         ],
         compiler_params=pltpu.CompilerParams(
-            collective_id=0, has_side_effects=True, vmem_limit_bytes=52 * 1024 * 1024
+            collective_id=0, has_side_effects=True, vmem_limit_bytes=64 * 1024 * 1024
         ),
         cost_estimate=pl.CostEstimate(flops=2_000_000_000, bytes_accessed=6_000_000, transcendentals=300_000),
         name="kv_backward",
@@ -392,7 +581,7 @@
         k_gain.reshape(1, head_dim),
         q_gain.reshape(1, head_dim),
     )
-    return (d_weight[:rows_dev], d_gain[0])
+    return (d_weight[:rows_dev].astype(F32), d_gain[0])
 
 
 def solution(mesh):
@@ -408,8 +597,10 @@
         P(),
     )
     out_specs = (P("fsdp", None), P())
+    data = mesh.shape["dp"]
+    tall = max(n for n in range(1, math.isqrt(data) + 1) if data % n == 0)
     return jax.shard_map(
-        functools.partial(shards, mesh.shape["dp"], mesh.shape["fsdp"]),
+        functools.partial(shards, (tall, data // tall), mesh.shape["fsdp"]),
         mesh=mesh,
         in_specs=in_specs,
         out_specs=out_specs,

time: 61.1 us -> 52.9 us (0.87)
  local copies, waits for them, and re-layouts: 8.87 us -> 1.19 us
  Pallas kernels: 51.2 us -> 49 us
  other arithmetic: 0 us -> 1.85 us
    unnamed x17 -> x0, local copies, waits for them, and re-layouts: 8.36 us -> none
    pallas_call x1, Pallas kernels: 51.2 us -> 49 us  [shards(): pl.pallas_call(functools.partial(body, grid, owners), out_shape=(jax.Shap...]
    convert_element_type x0 -> x1, other arithmetic: none -> 1.85 us  [shards(): return (d_weight[:rows_dev].astype(F32), d_gain[0])]
    squeeze x1, local copies, waits for them, and re-layouts: 0.51 us -> 1.19 us  [shards(): return (d_weight[:rows_dev].astype(F32), d_gain[0])]
where the time goes in v2:
time: 52.9 us; the launch traced here: 52.7 us
  Pallas kernels  49 us (93%)
  other arithmetic  1.85 us (3%)
  local copies, waits for them, and re-layouts  1.19 us (2%)
  between operations  0.64 us (1%)
    pallas_call x1, Pallas kernels, shards(): pl.pallas_call(functools.partial(body, grid, owners), out_shape=(jax.Shap...  49 us
    convert_element_type x1, other arithmetic, shards(): return (d_weight[:rows_dev].astype(F32), d_gain[0])  1.85 us
    squeeze x1, local copies, waits for them, and re-layouts, shards(): return (d_weight[:rows_dev].astype(F32), d_gain[0])  1.19 us

profile of v2, /device:TPU:0, one launch (start us, length us, event | category | flops | bytes accessed | tf_op | source)
XLA Modules:
  0.0 52.7 jit_solution(15022897335899349590)
XLA Ops:
  0.6 49.0 %kv_backward.1 = (bf16[640,256]{1,0:T(8,128)(2,1)}, f32[8,128]{1,0:T(8,128)}) custom-call(bf16[256,5120]{1,0:T(8,128)(2,1)} %bitcast.7, bf16[256,1024]{1,0:T(8,128)(2,1)} %bitcast.8, bf16[256,1024]{1,0:T(8,128)(2,1)} %bitcast.9, f32[1,256]{1,0:T(1,128)} %advantage.1, s32[1,256]{1,0:T(1,128)} %selected.1, s32[1,256]{1,0:T(1,128)} %segment.1, ...), custom_call_target="tpu_custom_call" | custom-call | flops 2000000000 | bytes 6000000 | tf_op jit(solution)/shard_map/kv_backward/pallas_call | solution.py:512
  49.6 1.2 %slice_bitcast_fusion = f32[128]{0:T(128)} fusion(f32[8,128]{1,0:T(8,128)} %get-tuple-element.5), kind=kLoop, calls=%fused_computation | loop fusion | bytes 1024 | tf_op jit(solution)/shard_map/squeeze | solution.py:584
  50.8 1.9 %convert_element_type.3 = f32[640,256]{1,0:T(8,128)} convert(bf16[640,256]{1,0:T(8,128)(2,1)} %get-tuple-element.4) | non-fusion elementwise | flops 163840 | bytes 983040 | tf_op jit(solution)/shard_map/convert_element_type | solution.py:584

commit v3 on v2

--- a/solution.py
+++ b/solution.py
@@ -49,6 +49,10 @@
     u_raw,
     q_sel,
     c_sel,
+    q_sel_t,
+    c_sel_t,
+    probs_all,
+    dscore_all,
     allowed,
     kv_out,
     kv_own,
@@ -243,29 +247,47 @@
                 diag[k, 1, s, t].start()
                 ahead.append(diag[k, 1, s, t])
 
+    def prepare_head(h):
+        lanes = pl.ds(h * head_dim, head_dim)
+        rows_h = pl.ds(h * cap, cap)
+        query = dot(pick_b, q_raw[:, lanes])
+        query_scale = lax.rsqrt(jnp.mean(query * query, axis=-1, keepdims=True) + epsilon)
+        query = query * query_scale * qg_in[...]
+        q_sel[rows_h] = query.astype(BF16)
+        q_sel_t[:, rows_h] = query.T.astype(BF16)
+        grad = token_weight * dot(pick_b, u_raw[:, lanes])
+        c_sel[rows_h] = grad.astype(BF16)
+        c_sel_t[:, rows_h] = grad.T.astype(BF16)
+
+    def turn_own(j):
+        loads[j].wait()
+        hid_t[pl.ds(j * rows, rows), :length] = hid[0, :, pl.ds(j * rows, rows)].T
+
+    def turn_swapped(j):
+        swaps[j].wait()
+        hid_t[pl.ds(j * rows, rows), length:] = hid[1, :, pl.ds(j * rows, rows)].T
+
+    tasks = [functools.partial(prepare_head, h) for h in range(heads)]
+    tasks += [functools.partial(turn_own, j) for j in range(chips)]
+    tasks += [functools.partial(turn_swapped, j) for j in range(chips)]
+    events = []
     for k in range(1, chips):
-        forward(k)
+        events.append(functools.partial(forward, k))
         if k > 1:
-            forward_diag(k - 1)
-
+            events.append(functools.partial(forward_diag, k - 1))
+    if chips > 1:
+        events.append(functools.partial(forward_diag, chips - 1))
     load_q.wait()
     load_u.wait()
-    for h in range(heads):
-        lanes = pl.ds(h * head_dim, head_dim)
-        query = dot(pick_b, q_raw[:, lanes])
-        query_scale = lax.rsqrt(jnp.mean(query * query, axis=-1, keepdims=True) + epsilon)
-        q_sel[pl.ds(h * cap, cap)] = (query * query_scale * qg_in[...]).astype(BF16)
-        grad = dot(pick_b, u_raw[:, lanes])
-        c_sel[pl.ds(h * cap, cap)] = (token_weight * grad).astype(BF16)
-
-    if chips > 1:
-        forward_diag(chips - 1)
-    for j in range(chips):
-        loads[j].wait()
-        hid_t[pl.ds(j * rows, rows), :length] = hid[0, :, pl.ds(j * rows, rows)].T
-    for j in range(chips):
-        swaps[j].wait()
-        hid_t[pl.ds(j * rows, rows), length:] = hid[1, :, pl.ds(j * rows, rows)].T
+    done = 0
+    for n, event in enumerate(events):
+        until = len(tasks) * (n + 1) // (len(events) + 1)
+        for task in tasks[done:until]:
+            task()
+        done = until
+        event()
+    for task in tasks[done:]:
+        task()
 
     own_w.wait()
     for k in range(chips):
@@ -296,21 +318,18 @@
     k_hat = k_raw * k_scale
     k_norm = (k_hat * kg_in[...]).astype(BF16)
     values = key_value[:, head_dim:].astype(BF16)
-    d_key = jnp.zeros((length, head_dim), F32)
-    d_value = jnp.zeros((length, head_dim), F32)
     for h in range(heads // 2):
         pair = pl.ds(h * 2 * cap, 2 * cap)
-        q_pair = q_sel[pair]
-        c_pair = c_sel[pair]
-        expo = jnp.exp(dot_last(k_norm, q_pair) * scale) * allowed[...]
+        expo = jnp.exp(dot(k_norm, q_sel_t[:, pair]) * scale) * allowed[...]
         total = jnp.sum(expo, axis=0, keepdims=True)
         probs = expo * (1.0 / jnp.where(total > 0.0, total, 1.0))
         probs_b = probs.astype(BF16)
-        dprob = dot_last(values, c_pair)
+        probs_all[:, pair] = probs_b
+        dprob = dot(values, c_sel_t[:, pair])
         delta = jnp.sum(probs_b.astype(F32) * dprob, axis=0, keepdims=True)
-        dscore = (probs * (dprob - delta) * scale).astype(BF16)
-        d_key += dot(dscore, q_pair)
-        d_value += dot(probs_b, c_pair)
+        dscore_all[:, pair] = (probs * (dprob - delta) * scale).astype(BF16)
+    d_key = dot(dscore_all[...], q_sel[...])
+    d_value = dot(probs_all[...], c_sel[...])
     d_khat = d_key * kg_in[...]
     d_kraw = k_scale * (d_khat - k_hat * jnp.mean(d_khat * k_hat, axis=-1, keepdims=True))
     d_kv[0, :, :head_dim] = d_kraw.astype(BF16)
@@ -530,6 +549,10 @@
             pltpu.VMEM((length, heads * head_dim), BF16),
             pltpu.VMEM((heads * CAP, head_dim), BF16),
             pltpu.VMEM((heads * CAP, head_dim), BF16),
+            pltpu.VMEM((head_dim, heads * CAP), BF16),
+            pltpu.VMEM((head_dim, heads * CAP), BF16),
+            pltpu.VMEM((length, heads * CAP), BF16),
+            pltpu.VMEM((length, heads * CAP), BF16),
             pltpu.VMEM((length, 2 * CAP), F32),
             pltpu.VMEM((length, columns), F32),
             pltpu.VMEM((length, columns), F32),

time: 52.9 us -> 52.4 us (level)
  no operation moved by 1% of the time
where the time goes in v3:
time: 52.4 us; the launch traced here: 52.2 us
  Pallas kernels  48.5 us (93%)
  other arithmetic  1.85 us (4%)
  local copies, waits for them, and re-layouts  1.19 us (2%)
  between operations  0.64 us (1%)
    pallas_call x1, Pallas kernels, shards(): pl.pallas_call(functools.partial(body, grid, owners), out_shape=(jax.Shap...  48.5 us
    convert_element_type x1, other arithmetic, shards(): return (d_weight[:rows_dev].astype(F32), d_gain[0])  1.85 us
    squeeze x1, local copies, waits for them, and re-layouts, shards(): return (d_weight[:rows_dev].astype(F32), d_gain[0])  1.19 us

profile of v3, /device:TPU:0, one launch (start us, length us, event | category | flops | bytes accessed | tf_op | source)
XLA Modules:
  0.0 52.2 jit_solution(6901083482507343191)
XLA Ops:
  0.6 48.5 %kv_backward.1 = (bf16[640,256]{1,0:T(8,128)(2,1)}, f32[8,128]{1,0:T(8,128)}) custom-call(bf16[256,5120]{1,0:T(8,128)(2,1)} %bitcast.7, bf16[256,1024]{1,0:T(8,128)(2,1)} %bitcast.8, bf16[256,1024]{1,0:T(8,128)(2,1)} %bitcast.9, f32[1,256]{1,0:T(1,128)} %advantage.1, s32[1,256]{1,0:T(1,128)} %selected.1, s32[1,256]{1,0:T(1,128)} %segment.1, ...), custom_call_target="tpu_custom_call" | custom-call | flops 2000000000 | bytes 6000000 | tf_op jit(solution)/shard_map/kv_backward/pallas_call | solution.py:531
  49.2 1.2 %slice_bitcast_fusion = f32[128]{0:T(128)} fusion(f32[8,128]{1,0:T(8,128)} %get-tuple-element.5), kind=kLoop, calls=%fused_computation | loop fusion | bytes 1024 | tf_op jit(solution)/shard_map/squeeze | solution.py:607
  50.4 1.9 %convert_element_type.3 = f32[640,256]{1,0:T(8,128)} convert(bf16[640,256]{1,0:T(8,128)(2,1)} %get-tuple-element.4) | non-fusion elementwise | flops 163840 | bytes 983040 | tf_op jit(solution)/shard_map/convert_element_type | solution.py:607

commit v4 on v3

--- a/solution.py
+++ b/solution.py
@@ -382,10 +382,11 @@
                     )
                 )
         for t in range(1, wide):
+            whole = tall == 1
             nears[k, 0, t, 0] = begin(
                 remote(
-                    part.at[target, rows_of(place(0, t)), low],
-                    from_row.at[t, k - 1, :, low],
+                    part.at[target, rows_of(place(0, t))] if whole else part.at[target, rows_of(place(0, t)), low],
+                    from_row.at[t, k - 1] if whole else from_row.at[t, k - 1, :, low],
                     row_sem.at[0, 0, k - 1, t - 1],
                     row_sem.at[1, 0, k - 1, t - 1],
                     to_data(place(0, t)),
@@ -419,6 +420,8 @@
                     to_data(place(s, 0)),
                 )
             )
+        if tall == 1:
+            return
         for t in range(1, wide):
             sent = part[target, rows_of(place(0, t)), high].astype(F32)
             for s in range(1, tall):
@@ -507,6 +510,11 @@
     d_weight[...] = final[...]
 
 
+def widen(narrow, gain, d_weight, d_gain):
+    d_weight[...] = narrow[: d_weight.shape[0]].astype(F32)
+    d_gain[...] = gain[0]
+
+
 def shards(grid, owners, hidden, queries, upstream, advantage, selected, segment, w_kv, k_gain, q_gain):
     hidden_row = hidden[0]
     length, width = hidden_row.shape
@@ -515,6 +523,7 @@
     heads = queries.shape[2] // head_dim
     tall, wide = grid
     data = tall * wide
+    far = (2, owners // 2, tall - 1, wide - 1) if tall > 1 else (2, 1, 1, 1)
     unit = math.lcm(128, 16 * data)
     rows = -(-rows_dev // unit) * unit
     chips = owners // 2
@@ -576,11 +585,11 @@
             dma((2, chips)),
             dma((2, chips, max(wide - 1, 1))),
             dma((2, chips, max(tall - 1, 1))),
-            dma((2, chips, max(tall - 1, 1), max(wide - 1, 1))),
-            dma((2, chips, max(tall - 1, 1), max(wide - 1, 1))),
+            dma(far),
+            dma(far),
             dma((6,)),
-            dma((2, chips, max(tall - 1, 1), max(wide - 1, 1))),
-            dma((2, chips, max(tall - 1, 1), max(wide - 1, 1))),
+            dma(far),
+            dma(far),
             dma((2, 2, chips, max(wide - 1, 1))),
             dma((2, 2, chips, max(tall - 1, 1))),
             dma((2, chips)),
@@ -604,7 +613,17 @@
         k_gain.reshape(1, head_dim),
         q_gain.reshape(1, head_dim),
     )
-    return (d_weight[:rows_dev].astype(F32), d_gain[0])
+    return pl.pallas_call(
+        widen,
+        out_shape=(
+            jax.ShapeDtypeStruct((rows_dev, columns), F32),
+            jax.ShapeDtypeStruct((head_dim,), F32),
+        ),
+        in_specs=[vmem, vmem],
+        out_specs=(vmem, vmem),
+        compiler_params=pltpu.CompilerParams(vmem_limit_bytes=64 * 1024 * 1024),
+        name="widen",
+    )(d_weight, d_gain)
 
 
 def solution(mesh):
@@ -621,7 +640,7 @@
     )
     out_specs = (P("fsdp", None), P())
     data = mesh.shape["dp"]
-    tall = max(n for n in range(1, math.isqrt(data) + 1) if data % n == 0)
+    tall = 1
     return jax.shard_map(
         functools.partial(shards, (tall, data // tall), mesh.shape["fsdp"]),
         mesh=mesh,

time: 52.4 us -> 54.6 us (1.042)
  Pallas kernels: 48.5 us -> 53.8 us
  other arithmetic: 1.85 us -> 0 us
  local copies, waits for them, and re-layouts: 1.19 us -> 0 us
    pallas_call x1, Pallas kernels: 48.5 us -> 52 us  [shards(): pl.pallas_call(functools.partial(body, grid, owners), out_shape=(jax.Shap...]
    pallas_call x0 -> x1, Pallas kernels: none -> 1.86 us  [shards(): pl.pallas_call(widen, out_shape=(jax.ShapeDtypeStruct((rows_dev, columns)...]
    convert_element_type x1 -> x0, other arithmetic: 1.85 us -> none  [shards(): return (d_weight[:rows_dev].astype(F32), d_gain[0])]
    squeeze x1 -> x0, local copies, waits for them, and re-layouts: 1.19 us -> none  [shards(): return (d_weight[:rows_dev].astype(F32), d_gain[0])]
where the time goes in v4:
time: 54.6 us; the launch traced here: 54.5 us
  Pallas kernels  53.8 us (99%)
  between operations  0.64 us (1%)
    pallas_call x1, Pallas kernels, shards(): pl.pallas_call(functools.partial(body, grid, owners), out_shape=(jax.Shap...  52 us
    pallas_call x1, Pallas kernels, shards(): pl.pallas_call(widen, out_shape=(jax.ShapeDtypeStruct((rows_dev, columns)...  1.86 us

profile of v4, /device:TPU:0, one launch (start us, length us, event | category | flops | bytes accessed | tf_op | source)
XLA Modules:
  0.0 54.5 jit_solution(10632182089597688676)
XLA Ops:
  0.6 52.0 %kv_backward.1 = (bf16[640,256]{1,0:T(8,128)(2,1)}, f32[8,128]{1,0:T(8,128)}) custom-call(bf16[256,5120]{1,0:T(8,128)(2,1)} %bitcast.5, bf16[256,1024]{1,0:T(8,128)(2,1)} %bitcast.6, bf16[256,1024]{1,0:T(8,128)(2,1)} %bitcast.7, f32[1,256]{1,0:T(1,128)} %advantage.1, s32[1,256]{1,0:T(1,128)} %selected.1, s32[1,256]{1,0:T(1,128)} %segment.1, ...), custom_call_target="tpu_custom_call" | custom-call | flops 2000000000 | bytes 6000000 | tf_op jit(solution)/shard_map/kv_backward/pallas_call | solution.py:540
  52.6 1.9 %widen.1 = (f32[640,256]{1,0:T(8,128)}, f32[128]{0:T(128)}) custom-call(bf16[640,256]{1,0:T(8,128)(2,1)} %get-tuple-element.4.narrow, f32[8,128]{1,0:T(8,128)} %get-tuple-element.5.gain), custom_call_target="tpu_custom_call" | custom-call | tf_op jit(solution)/shard_map/widen/pallas_call | solution.py:616
